TPU v7x, 32 devices: a whole 2x2x4 slice. The times are simulated.
32 devices in a mesh: groups: 2 (over y), feat: 4 (over z), dp: 4 (over x, core).
Axes of the slice: x: 2, y: 2, z: 4, core: 2. Of those that a mesh axis runs over, the one named last changes fastest.
Arguments:
- features: bfloat16 [2048, 8192], P(('groups', 'dp'), 'feat'), parts along dimension 0, may hold values from -6 to 6
- bn_gain: float32 [8192], P('feat'), may hold values from 0.1 to 1.9
- bn_shift: float32 [8192], P('feat'), may hold values from -0.5 to 0.5
- weight: bfloat16 [8192, 8192], P('feat'), may hold values from -2 to 2
Outputs:
- covariance: float32 [16384, 8192], P(('groups', 'dp'), 'feat'), parts along dimension 0
- grad_in: bfloat16 [2048, 8192], P(('groups', 'dp'), 'feat'), parts along dimension 0
There are 2 independent parts, one for each index of `groups`. A program takes and returns all parts, laid end to end along the dimension named above; an argument that names none is the same for every part. Nothing has to cross between parts.
All inputs are finite; a program needn't handle non-finite values.
Results may differ from a plain program's by a relative error of at most 0.014.
Values may be sent and summed in bfloat16 or wider, within the bound.
A program may use at most 256 MiB of HBM per device.

v0:
```python
import jax
import jax.numpy as jnp
from jax import lax
from jax.sharding import PartitionSpec as P


def whole_rows(centered):
    return lax.all_gather(centered, "feat", axis=1, tiled=True)


def shards(features, bn_gain, bn_shift, weight):
    dp_count = lax.axis_size("dp")
    feat_count = lax.axis_size("feat")
    local_rows = features.shape[0]
    images = local_rows * dp_count
    hidden = features.astype(jnp.float32)
    col_sums, col_squares = lax.psum((jnp.sum(hidden, 0), jnp.sum(hidden * hidden, 0)), "dp")
    mean_h = col_sums / images
    var_h = col_squares / images - mean_h * mean_h
    normed = (hidden - mean_h) * lax.rsqrt(var_h + 1e-05) * bn_gain + bn_shift
    activated = jnp.maximum(normed, 0.0).astype(jnp.bfloat16)
    partial_value = jnp.dot(activated, weight, preferred_element_type=jnp.float32)
    projected = lax.psum_scatter(partial_value, "feat", scatter_dimension=1, tiled=True).astype(
        jnp.bfloat16
    )
    proj_f = projected.astype(jnp.float32)
    proj_mean = lax.psum(jnp.sum(proj_f, 0), "dp") / images
    centered = (proj_f - proj_mean).astype(jnp.bfloat16)
    cent_f = centered.astype(jnp.float32)
    width_f = centered.shape[1]
    width_x = width_f * feat_count // dp_count
    cent_full = None
    cent_full = whole_rows(centered)
    cent_x = lax.all_to_all(cent_full, "dp", split_axis=1, concat_axis=0, tiled=True)
    piece = lax.all_gather(centered, "dp", axis=0, tiled=True)
    cov_tile = lax.dot_general(
        cent_x, piece, (((0,), (0,)), ((), ())), preferred_element_type=jnp.float32
    )
    piece_f = piece.astype(jnp.float32)
    cov_tile, sq_sum = (cov_tile, jnp.sum(piece_f * piece_f, 0))
    covariance = cov_tile / (images - 1)
    proj_var = sq_sum / (images - 1)
    spread = jnp.sqrt(proj_var + 0.0001)
    row_ids = lax.axis_index("dp") * width_x + jnp.arange(width_x, dtype=jnp.int32)[:, None]
    col_ids = lax.axis_index("feat") * width_f + jnp.arange(width_f, dtype=jnp.int32)[None, :]
    off_diag = jnp.where(row_ids == col_ids, 0.0, covariance).astype(jnp.bfloat16)
    mixed = jnp.dot(
        cent_full,
        lax.all_gather(off_diag, "dp", axis=0, tiled=True),
        preferred_element_type=jnp.float32,
    )
    scale_up = images / (images - 1)
    active = jnp.where(spread < 1.0, 1.0 / spread, 0.0)
    grad_proj = (4.0 * scale_up * mixed - 25.0 * scale_up * active * cent_f).astype(jnp.bfloat16)
    grad_in = lax.dot_general(
        lax.all_gather(grad_proj, "feat", axis=1, tiled=True),
        weight,
        (((1,), (1,)), ((), ())),
        preferred_element_type=jnp.float32,
    )
    return (covariance, grad_in.astype(jnp.bfloat16))


def solution(mesh):
    in_specs = (P(("groups", "dp"), "feat"), P("feat"), P("feat"), P("feat", None))
    out_specs = (P(("groups", "dp"), "feat"), P(("groups", "dp"), "feat"))
    return jax.shard_map(shards, mesh=mesh, in_specs=in_specs, out_specs=out_specs, check_vma=False)
```

profile of v0, /device:TPU:0, one launch (start us, length us, event | category | flops | bytes accessed | tf_op | source)
XLA Modules:
  0.0 694.4 jit_solution(14080801374418411626)
XLA Ops:
  7.2 0.0 reduce-scatter.2.cloned.1.call-start
  7.2 1.5 convert_reduce_fusion
  8.7 12.7 %all-reduce = (f32[2048]{0:T(1024)S(1)}, f32[2048]{0:T(1024)S(1)}) all-reduce(f32[2048]{0:T(1024)S(1)} %get-tuple-element.3, f32[2048]{0:T(1024)S(1)} %get-tuple-element.2), channel_id=1, replica_groups=mesh['groups'=2,'feat'=4,'dp'=4] {'dp'}, use_global_device_ids=true, to_apply=%region_3.0 | all-reduce | flops 4096 | bytes 32768 | tf_op jit(solution)/shard_map/psum | solution.py:17
  21.4 17.4 %fusion.9 = f32[256,8192]{1,0:T(8,128)} fusion(bf16[2048,8192]{1,0:T(8,128)(2,1)} %param.7, bf16[256,2048]{1,0:T(8,128)(2,1)} %param.4, f32[2048]{0:T(1024)} %param.6, f32[2048]{0:T(1024)} %param.5, f32[2048]{0:T(1024)S(1)} %get-tuple-element.7, f32[2048]{0:T(1024)S(1)} %get-tuple-element.6), kind=kOutput, calls=%fused_computation.20 | convolution fusion | flops 8593604608 | bytes 43024384 | tf_op jit(solution)/shard_map/dot_general | solution.py:22
  38.9 0.0 all-gather.5.cloned.1.call-start
  38.9 144.9 %reduce-scatter.2.cloned.1.call-done = f32[256,2048]{1,0:T(8,128)} async-done(((f32[256,8192]{1,0:T(8,128)}), f32[256,2048]{1,0:T(8,128)}) %reduce-scatter.2.cloned.1.call-update) | async-done | bytes 2097168 | tf_op jit(solution)/shard_map/reduce_scatter | solution.py:23
  183.8 1.7 convert_reduce_fusion.1
  185.5 6.5 psum.23
  192.0 2.7 fusion.2
  194.8 0.0 all-gather.7.cloned.1.call-start
  194.9 0.7 all-gather.7.cloned.1.call-update
  195.6 80.5 %all-gather.5.cloned.1.call-done = bf16[256,8192]{1,0:T(8,128)(2,1)} async-done(((bf16[256,2048]{1,0:T(8,128)(2,1)}), bf16[256,8192]{1,0:T(8,128)(2,1)}) %all-gather.5.cloned.1.call-update) | async-done | bytes 4194320 | tf_op jit(solution)/shard_map/all_gather | solution.py:8
  276.0 4.8 copy.9
  280.8 4.9 all-to-all-start
  285.8 0.0 all-gather.9.cloned.1.call-start
  285.8 46.1 %all-gather.7.cloned.1.call-done = bf16[1024,2048]{1,0:T(8,128)(2,1)} async-done(((bf16[256,2048]{1,0:T(8,128)(2,1)}), bf16[1024,2048]{1,0:T(8,128)(2,1)}) %all-gather.7.cloned.1.call-update) | async-done | bytes 4194320 | tf_op jit(solution)/shard_map/all_gather | solution.py:35
  332.0 22.7 %all-to-all-done = bf16[256,4,2048]{2,0,1:T(8,128)(2,1)} async-done(((bf16[256,4,2048]{2,0,1:T(8,128)(2,1)}), bf16[256,4,2048]{2,0,1:T(8,128)(2,1)}, u32[]{:S(2)}, u32[]{:S(2)}) %all-to-all-start) | async-done | bytes 4194336 | tf_op jit(solution)/shard_map/all_to_all | solution.py:34
  354.6 17.6 %select_convert_fusion = (bf16[2048,2048]{1,0:T(8,128)(2,1)}, f32[2048,2048]{1,0:T(8,128)}) fusion(s32[2048]{0:T(1024)S(1)} %get-tuple-element.10, s32[2048]{0:T(1024)S(1)} %get-tuple-element.11, bf16[1024,2048]{1,0:T(8,128)(2,1)} %bitcast.1, bf16[1024,2048]{1,0:T(8,128)(2,1)} %all-gather.7.cloned.1.call-done), kind=kOutput, calls=%fused_computation | convolution fusion | flops 8602517504 | bytes 33570816 | tf_op jit(solution)/shard_map/dot_general | solution.py:36
  372.3 0.2 all-gather.11.cloned.1.call-start
  372.5 3.1 multiply_reduce_fusion
  375.7 197.5 %all-gather.9.cloned.1.call-done = bf16[8192,2048]{1,0:T(8,128)(2,1)} async-done(((bf16[2048,2048]{1,0:T(8,128)(2,1)}), bf16[8192,2048]{1,0:T(8,128)(2,1)}) %all-gather.9.cloned.1.call-update) | async-done | bytes 33554448 | tf_op jit(solution)/shard_map/all_gather | solution.py:49
  573.2 17.0 %fusion.1 = bf16[256,2048]{1,0:T(8,128)(2,1)} fusion(bf16[256,8192]{1,0:T(8,128)(2,1)} %all-gather.5.cloned.1.call-done, bf16[8192,2048]{1,0:T(8,128)(2,1)} %all-gather.9.cloned.1.call-done, bf16[256,2048]{1,0:T(8,128)(2,1)S(1)} %copy-done, f32[2048]{0:T(1024)S(1)} %select_multiply_fusion), kind=kOutput, calls=%fused_computation.11 | convolution fusion | flops 8592556032 | bytes 39854080 | tf_op jit(solution)/shard_map/dot_general | solution.py:47
  590.3 80.9 %all-gather.11.cloned.1.call-done = bf16[256,8192]{1,0:T(8,128)(2,1)} async-done(((bf16[256,2048]{1,0:T(8,128)(2,1)}), bf16[256,8192]{1,0:T(8,128)(2,1)}) %all-gather.11.cloned.1.call-update) | async-done | bytes 4194320 | tf_op jit(solution)/shard_map/all_gather | solution.py:56
  671.2 16.6 %convolution_convert_fusion = bf16[256,2048]{1,0:T(8,128)(2,1)} fusion(bf16[256,8192]{1,0:T(8,128)(2,1)} %all-gather.11.cloned.1.call-done, bf16[2048,8192]{1,0:T(8,128)(2,1)} %param.7), kind=kOutput, calls=%fused_computation.12 | convolution fusion | flops 8590458880 | bytes 38797312 | tf_op jit(solution)/shard_map/dot_general | solution.py:55
  (10 shorter events, 0.1 us)
Async XLA Ops:
  7.2 176.7 %reduce-scatter.2.cloned.1.call-start = ((), (), s32[]{:S(2)}) async-start(), calls=%async_computation.2 | async-start | bytes 10485760 | tf_op jit(solution)/shard_map/reduce_scatter | solution.py:23
  38.9 237.2 %all-gather.5.cloned.1.call-start = ((), (), s32[]{:S(2)}) async-start(), calls=%async_computation.3 | async-start | bytes 5242880 | tf_op jit(solution)/shard_map/all_gather | solution.py:8
  194.8 137.1 %all-gather.7.cloned.1.call-start = ((), (), s32[]{:S(2)}) async-start(), calls=%async_computation.4 | async-start | bytes 5242880 | tf_op jit(solution)/shard_map/all_gather | solution.py:35
  280.8 73.8 %all-to-all-start = ((bf16[256,4,2048]{2,0,1:T(8,128)(2,1)}), bf16[256,4,2048]{2,0,1:T(8,128)(2,1)}, u32[]{:S(2)}, u32[]{:S(2)}) async-start(bf16[256,4,2048]{2,0,1:T(8,128)(2,1)} %bitcast.14), calls=%async_computation.1 | async-start | bytes 8388608 | tf_op jit(solution)/shard_map/all_to_all | solution.py:34
  285.8 287.4 %all-gather.9.cloned.1.call-start = ((), (), s32[]{:S(2)}) async-start(), calls=%async_computation.5 | async-start | bytes 41943040 | tf_op jit(solution)/shard_map/all_gather | solution.py:49
  372.3 200.9 %copy-start = (bf16[256,2048]{1,0:T(8,128)(2,1)S(1)}, bf16[256,2048]{1,0:T(8,128)(2,1)}, u32[]{:S(2)}) copy-start(bf16[256,2048]{1,0:T(8,128)(2,1)} %fusion.2) | copy-start | bytes 3145732
  372.3 298.9 %all-gather.11.cloned.1.call-start = ((), (), s32[]{:S(2)}) async-start(), calls=%async_computation.6 | async-start | bytes 5242880 | tf_op jit(solution)/shard_map/all_gather | solution.py:56
Sparse Core Ops, SparseCore 0:
  39.0 144.7 reduce-scatter.1
  194.9 81.0 all-gather.4
  278.2 53.7 all-gather.6
  372.4 200.7 all-gather.8
  590.4 80.7 all-gather.10
where the time goes:
time: 695 us; the launch traced here: 694 us
  waiting for transfers between devices  573 us (82%)
  matrix products  68.7 us (10%)
  blocking collectives  19.2 us (3%)
  between operations  13.8 us (2%)
  other arithmetic  9.16 us (1%)
    all_gather x1, waiting for transfers between devices, shards(): lax.all_gather(off_diag, 'dp', axis=0, tiled=True)  198 us
    reduce_scatter x1, waiting for transfers between devices, shards(): lax.psum_scatter(partial_value, 'feat', scatter_dimension=1, tiled=True)  145 us
    all_gather x1, waiting for transfers between devices, shards(): lax.all_gather(grad_proj, 'feat', axis=1, tiled=True)  80.9 us
    all_gather x1, waiting for transfers between devices, whole_rows(): return lax.all_gather(centered, 'feat', axis=1, tiled=True)  80.5 us
    all_gather x1, waiting for transfers between devices, shards(): piece = lax.all_gather(centered, 'dp', axis=0, tiled=True)  46.1 us
    all_to_all x1, waiting for transfers between devices, shards(): lax.all_to_all(cent_full, 'dp', split_axis=1, concat_axis=0, tiled=True)  22.7 us
    dot_general x1, matrix products, shards(): lax.dot_general(cent_x, piece, (((0,), (0,)), ((), ())), preferred_elemen...  17.6 us
    dot_general x1, matrix products, shards(): jnp.dot(activated, weight, preferred_element_type=jnp.float32)  17.4 us
  transfers between devices with their start and end apart: 6, of which 6 were waited for; matrix products, arithmetic and copies ran while one was open for 1% of the time, Pallas kernels for 0%

commit v1 on v0

--- a/solution.py
+++ b/solution.py
@@ -32,7 +32,12 @@
     cent_full = None
     cent_full = whole_rows(centered)
     cent_x = lax.all_to_all(cent_full, "dp", split_axis=1, concat_axis=0, tiled=True)
-    piece = lax.all_gather(centered, "dp", axis=0, tiled=True)
+    ring = [centered]
+    for hop in range(3):
+        ring.append(lax.ppermute(ring[-1], "dp", [(dev, (dev + 1) % 4) for dev in range(4)]))
+    piece = jnp.roll(
+        jnp.concatenate(ring[::-1], axis=0), (lax.axis_index("dp") + 1) * ring[0].shape[0], axis=0
+    )
     cov_tile = lax.dot_general(
         cent_x, piece, (((0,), (0,)), ((), ())), preferred_element_type=jnp.float32
     )

time: 695 us -> 673 us (0.968)
  waiting for transfers between devices: 573 us -> 537 us
  local copies, waits for them, and re-layouts: 4.79 us -> 16.4 us
    all_gather x1 -> x0, waiting for transfers between devices: 46.1 us -> none  [shards(): piece = lax.all_gather(centered, 'dp', axis=0, tiled=True)]
    ppermute x0 -> x3, waiting for transfers between devices: none -> 28.8 us  [shards(): lax.ppermute(ring[-1], 'dp', [(dev, (dev + 1) % 4) for dev in range(4)])]
    all_gather x1, waiting for transfers between devices: 80.5 us -> 52.4 us  [whole_rows(): return lax.all_gather(centered, 'feat', axis=1, tiled=True)]
    unnamed x2 -> x10, local copies, waits for them, and re-layouts: 0.01 us -> 11.6 us
    all_to_all x1, waiting for transfers between devices: 22.7 us -> 34.3 us  [shards(): lax.all_to_all(cent_full, 'dp', split_axis=1, concat_axis=0, tiled=True)]
  transfers between devices with their start and end apart: 6 -> 8, of which waited for: 6 -> 7; matrix products, arithmetic and copies ran while one was open for 1% -> 3% of each run, Pallas kernels for 0% -> 0%
where the time goes in v1:
time: 673 us; the launch traced here: 672 us
  waiting for transfers between devices  537 us (80%)
  matrix products  68.8 us (10%)
  blocking collectives  19.2 us (3%)
  local copies, waits for them, and re-layouts  16.4 us (2%)
  between operations  13.9 us (2%)
  other arithmetic  11.4 us (2%)
    all_gather x1, waiting for transfers between devices, shards(): lax.all_gather(off_diag, 'dp', axis=0, tiled=True)  196 us
    reduce_scatter x1, waiting for transfers between devices, shards(): lax.psum_scatter(partial_value, 'feat', scatter_dimension=1, tiled=True)  145 us
    all_gather x1, waiting for transfers between devices, shards(): lax.all_gather(grad_proj, 'feat', axis=1, tiled=True)  80.9 us
    all_gather x1, waiting for transfers between devices, whole_rows(): return lax.all_gather(centered, 'feat', axis=1, tiled=True)  52.4 us
    all_to_all x1, waiting for transfers between devices, shards(): lax.all_to_all(cent_full, 'dp', split_axis=1, concat_axis=0, tiled=True)  34.3 us
    ppermute x3, waiting for transfers between devices, shards(): lax.ppermute(ring[-1], 'dp', [(dev, (dev + 1) % 4) for dev in range(4)])  28.8 us
    dot_general x1, matrix products, shards(): lax.dot_general(cent_x, piece, (((0,), (0,)), ((), ())), preferred_elemen...  17.7 us
    dot_general x1, matrix products, shards(): jnp.dot(activated, weight, preferred_element_type=jnp.float32)  17.4 us
  transfers between devices with their start and end apart: 8, of which 7 were waited for; matrix products, arithmetic and copies ran while one was open for 3% of the time, Pallas kernels for 0%

profile of v1, /device:TPU:0, one launch (start us, length us, event | category | flops | bytes accessed | tf_op | source)
XLA Modules:
  0.0 672.1 jit_solution(281793774429425343)
XLA Ops:
  7.2 1.5 convert_reduce_fusion
  8.7 12.7 %all-reduce = (f32[2048]{0:T(1024)S(1)}, f32[2048]{0:T(1024)S(1)}) all-reduce(f32[2048]{0:T(1024)S(1)} %get-tuple-element.3, f32[2048]{0:T(1024)S(1)} %get-tuple-element.2), channel_id=1, replica_groups=mesh['groups'=2,'feat'=4,'dp'=4] {'dp'}, use_global_device_ids=true, to_apply=%region_3.0 | all-reduce | flops 4096 | bytes 32768 | tf_op jit(solution)/shard_map/psum | solution.py:17
  21.4 17.4 %fusion.10 = f32[256,8192]{1,0:T(8,128)} fusion(bf16[2048,8192]{1,0:T(8,128)(2,1)} %param.7, bf16[256,2048]{1,0:T(8,128)(2,1)} %param.4, f32[2048]{0:T(1024)} %param.6, f32[2048]{0:T(1024)} %param.5, f32[2048]{0:T(1024)S(1)} %get-tuple-element.7, f32[2048]{0:T(1024)S(1)} %get-tuple-element.6), kind=kOutput, calls=%fused_computation.21 | convolution fusion | flops 8593604608 | bytes 43024384 | tf_op jit(solution)/shard_map/dot_general | solution.py:22
  38.9 144.9 %reduce-scatter.2.cloned.1.call-done = f32[256,2048]{1,0:T(8,128)} async-done(((f32[256,8192]{1,0:T(8,128)}), f32[256,2048]{1,0:T(8,128)}) %reduce-scatter.2.cloned.1.call-update) | async-done | bytes 2097168 | tf_op jit(solution)/shard_map/reduce_scatter | solution.py:23
  183.8 1.7 convert_reduce_fusion.1
  185.5 6.5 psum.23
  192.0 2.7 fusion.3
  194.9 14.4 %collective-permute-done = bf16[256,2048]{1,0:T(8,128)(2,1)S(1)} collective-permute-done((bf16[256,2048]{1,0:T(8,128)(2,1)}, bf16[256,2048]{1,0:T(8,128)(2,1)S(1)}, u32[]{:S(2)}, u32[]{:S(2)}) %collective-permute-start) | collective-permute-done | bytes 1048608 | tf_op jit(solution)/shard_map/ppermute | solution.py:37
  209.3 14.3 %collective-permute-done.1 = bf16[256,2048]{1,0:T(8,128)(2,1)} collective-permute-done((bf16[256,2048]{1,0:T(8,128)(2,1)S(1)}, bf16[256,2048]{1,0:T(8,128)(2,1)}, u32[]{:S(2)}, u32[]{:S(2)}) %collective-permute-start.1) | collective-permute-done | bytes 1048608 | tf_op jit(solution)/shard_map/ppermute | solution.py:37
  223.6 52.4 %all-gather.4.cloned.1.call-done = bf16[256,8192]{1,0:T(8,128)(2,1)} async-done(((bf16[256,2048]{1,0:T(8,128)(2,1)}), bf16[256,8192]{1,0:T(8,128)(2,1)}) %all-gather.4.cloned.1.call-update) | async-done | bytes 4194320 | tf_op jit(solution)/shard_map/all_gather | solution.py:8
  276.0 4.8 copy.9
  280.8 4.8 all-to-all-start
  285.8 2.4 constant_dynamic-update-slice_fusion.7
  288.2 2.4 constant_dynamic-update-slice_fusion.6
  292.8 2.3 constant_dynamic-update-slice_fusion.3
  295.1 2.3 constant_dynamic-update-slice_fusion.2
  298.5 1.1 constant_dynamic-update-slice_fusion
  299.6 34.3 %all-to-all-done = bf16[256,4,2048]{2,0,1:T(8,128)(2,1)} async-done(((bf16[256,4,2048]{2,0,1:T(8,128)(2,1)}), bf16[256,4,2048]{2,0,1:T(8,128)(2,1)}, u32[]{:S(2)}, u32[]{:S(2)}) %all-to-all-start) | async-done | bytes 4194336 | tf_op jit(solution)/shard_map/all_to_all | solution.py:34
  333.9 17.7 %select_convert_fusion = (bf16[2048,2048]{1,0:T(8,128)(2,1)}, f32[2048,2048]{1,0:T(8,128)}) fusion(s32[2048]{0:T(1024)S(1)} %get-tuple-element.10, s32[2048]{0:T(1024)S(1)} %get-tuple-element.11, bf16[1024,2048]{1,0:T(8,128)(2,1)} %bitcast.1, bf16[2048,2048]{1,0:T(8,128)(2,1)} %constant_dynamic-update-slice_fusion, s32[]{:T(128)S(6)} %select_n.26), kind=kOutput, calls=%fused_computation | convolution fusion | flops 8602517504 | bytes 33570820 | tf_op jit(solution)/shard_map/dot_general | solution.py:41
  351.8 3.1 multiply_reduce_fusion
  355.0 195.9 %all-gather.6.cloned.1.call-done = bf16[8192,2048]{1,0:T(8,128)(2,1)} async-done(((bf16[2048,2048]{1,0:T(8,128)(2,1)}), bf16[8192,2048]{1,0:T(8,128)(2,1)}) %all-gather.6.cloned.1.call-update) | async-done | bytes 33554448 | tf_op jit(solution)/shard_map/all_gather | solution.py:54
  550.9 17.0 %fusion.2 = bf16[256,2048]{1,0:T(8,128)(2,1)} fusion(bf16[256,8192]{1,0:T(8,128)(2,1)} %all-gather.4.cloned.1.call-done, bf16[8192,2048]{1,0:T(8,128)(2,1)} %all-gather.6.cloned.1.call-done, bf16[256,2048]{1,0:T(8,128)(2,1)S(1)} %copy-done.1, f32[2048]{0:T(1024)S(1)} %select_multiply_fusion), kind=kOutput, calls=%fused_computation.12 | convolution fusion | flops 8592556032 | bytes 39854080 | tf_op jit(solution)/shard_map/dot_general | solution.py:52
  568.0 80.9 %all-gather.8.cloned.1.call-done = bf16[256,8192]{1,0:T(8,128)(2,1)} async-done(((bf16[256,2048]{1,0:T(8,128)(2,1)}), bf16[256,8192]{1,0:T(8,128)(2,1)}) %all-gather.8.cloned.1.call-update) | async-done | bytes 4194320 | tf_op jit(solution)/shard_map/all_gather | solution.py:61
  648.9 16.6 %convolution_convert_fusion = bf16[256,2048]{1,0:T(8,128)(2,1)} fusion(bf16[256,8192]{1,0:T(8,128)(2,1)} %all-gather.8.cloned.1.call-done, bf16[2048,8192]{1,0:T(8,128)(2,1)} %param.7), kind=kOutput, calls=%fused_computation.13 | convolution fusion | flops 8590458880 | bytes 38797312 | tf_op jit(solution)/shard_map/dot_general | solution.py:60
  (23 shorter events, 3.8 us)
Async XLA Ops:
  7.2 176.7 %reduce-scatter.2.cloned.1.call-start = ((), (), s32[]{:S(2)}) async-start(), calls=%async_computation.2 | async-start | bytes 10485760 | tf_op jit(solution)/shard_map/reduce_scatter | solution.py:23
  38.9 237.2 %all-gather.4.cloned.1.call-start = ((), (), s32[]{:S(2)}) async-start(), calls=%async_computation.3 | async-start | bytes 5242880 | tf_op jit(solution)/shard_map/all_gather | solution.py:8
  194.8 14.5 %collective-permute-start = (bf16[256,2048]{1,0:T(8,128)(2,1)}, bf16[256,2048]{1,0:T(8,128)(2,1)S(1)}, u32[]{:S(2)}, u32[]{:S(2)}) collective-permute-start(bf16[256,2048]{1,0:T(8,128)(2,1)} %fusion.3), channel_id=1, source_target_pairs={{0,1},{1,2},{2,3},{3,0},{4,5},{5,6},{6,7},{7,4},{8,9},{9,10},{10,1... | collective-permute-start | bytes 3145736 | tf_op jit(solution)/shard_map/ppermute | solution.py:37
  209.3 14.3 %collective-permute-start.1 = (bf16[256,2048]{1,0:T(8,128)(2,1)S(1)}, bf16[256,2048]{1,0:T(8,128)(2,1)}, u32[]{:S(2)}, u32[]{:S(2)}) collective-permute-start(bf16[256,2048]{1,0:T(8,128)(2,1)S(1)} %collective-permute-done), channel_id=1, source_target_pairs={{0,1},{1,2},{2,3},{3,0},{4,5},{5,6},{6,7},{7,4},{8,9},{9,10},{10,1... | collective-permute-start | bytes 3145736 | tf_op jit(solution)/shard_map/ppermute | solution.py:37
  223.6 62.1 %collective-permute-start.2 = (bf16[256,2048]{1,0:T(8,128)(2,1)}, bf16[256,2048]{1,0:T(8,128)(2,1)}, u32[]{:S(2)}, u32[]{:S(2)}) collective-permute-start(bf16[256,2048]{1,0:T(8,128)(2,1)} %collective-permute-done.1), channel_id=1, source_target_pairs={{0,1},{1,2},{2,3},{3,0},{4,5},{5,6},{6,7},{7,4},{8,9},{9,10},{10,1... | collective-permute-start | bytes 3145736 | tf_op jit(solution)/shard_map/ppermute | solution.py:37
  280.8 53.1 %all-to-all-start = ((bf16[256,4,2048]{2,0,1:T(8,128)(2,1)}), bf16[256,4,2048]{2,0,1:T(8,128)(2,1)}, u32[]{:S(2)}, u32[]{:S(2)}) async-start(bf16[256,4,2048]{2,0,1:T(8,128)(2,1)} %bitcast.13), calls=%async_computation.1 | async-start | bytes 8388608 | tf_op jit(solution)/shard_map/all_to_all | solution.py:34
  285.7 6.0 copy-start
  285.7 265.2 %all-gather.6.cloned.1.call-start = ((), (), s32[]{:S(2)}) async-start(), calls=%async_computation.4 | async-start | bytes 41943040 | tf_op jit(solution)/shard_map/all_gather | solution.py:54
  351.6 199.3 %copy-start.1 = (bf16[256,2048]{1,0:T(8,128)(2,1)S(1)}, bf16[256,2048]{1,0:T(8,128)(2,1)}, u32[]{:S(2)}) copy-start(bf16[256,2048]{1,0:T(8,128)(2,1)} %fusion.3) | copy-start | bytes 3145732
  351.6 297.3 %all-gather.8.cloned.1.call-start = ((), (), s32[]{:S(2)}) async-start(), calls=%async_computation.5 | async-start | bytes 5242880 | tf_op jit(solution)/shard_map/all_gather | solution.py:61
Sparse Core Ops, SparseCore 0:
  39.0 144.7 reduce-scatter.1
  194.9 81.0 all-gather.3
  351.7 199.1 all-gather.5
  568.1 80.7 all-gather.7
